TPU v7x, 256 devices: a whole 4x4x8 slice. The times are simulated.
256 devices in a mesh: rows: 4 (over x), chan: 8 (over y, z_lo), filt: 8 (over z_hi, core).
Axes of the slice: x: 4, y: 4, z: 8 (z_hi: 4, z_lo: 2; z = z_hi * 2 + z_lo), core: 2. Of those that a mesh axis runs over, the one named last changes fastest.
Arguments:
- images: bfloat16 [16, 2048, 2048], P('rows', 'chan', 'filt'), may hold values from -6 to 6
- first_weight: bfloat16 [2048, 1024], P('chan', 'filt'), may hold values from -0.125 to 0.125
- group_weight: bfloat16 [3, 3, 32, 1024], P(None, None, None, 'filt'), may hold values from -0.375 to 0.375
- third_weight: bfloat16 [1024, 2048], P('chan', 'filt'), may hold values from -0.1875 to 0.1875
- out_grad: bfloat16 [16, 2048, 2048], P('rows', 'chan', 'filt'), may hold values from -6 to 6
Outputs:
- block_out: bfloat16 [16, 2048, 2048], P('rows', 'chan', 'filt')
- images_grad: float32 [16, 2048, 2048], P('rows', 'chan', 'filt')
- first_grad: float32 [2048, 1024], P('chan', 'filt')
- group_grad: float32 [3, 3, 32, 1024], P(None, None, None, 'filt')
- third_grad: float32 [1024, 2048], P('chan', 'filt')
All inputs are finite; a program needn't handle non-finite values.
Results may differ from a plain program's by a relative error of at most 0.006.
Values may be sent and summed in bfloat16 or wider, within the bound.
No kernel may reach another device: no remote copies, remote signals or barrier semaphores. Data moves between devices by JAX's collectives and lax.ppermute only.
A program may use at most 128 MiB of HBM per device.

v0:
```python
import jax
import jax.numpy as jnp
from jax import lax
from jax.sharding import PartitionSpec as P


def extended(block, sides, width):
    for axis, dim in sides:
        count = lax.axis_size(axis)
        forward = [(i, i + 1) for i in range(count - 1)]
        backward = [(target, source) for source, target in forward]
        low = lax.ppermute(
            lax.slice_in_dim(block, block.shape[dim] - width, None, axis=dim), axis, forward
        )
        high = lax.ppermute(lax.slice_in_dim(block, 0, width, axis=dim), axis, backward)
        block = jnp.concatenate([low, block, high], axis=dim)
    return block


def silu_slope(values):
    logistic = jax.nn.sigmoid(values)
    return logistic * (1.0 + values * (1.0 - logistic))


def group_conv(padded, kernel, groups_here):
    result = lax.conv_general_dilated(
        padded[None],
        kernel,
        (1, 1),
        "VALID",
        dimension_numbers=("NHWC", "HWIO", "NHWC"),
        feature_group_count=groups_here,
        preferred_element_type=jnp.float32,
    )
    return result[0]


def transposed_kernel(kernel, group_size, groups_here):
    pieces = kernel.reshape(3, 3, group_size, groups_here, group_size)
    swapped = jnp.transpose(pieces, (0, 1, 4, 3, 2)).reshape(
        3, 3, group_size, groups_here * group_size
    )
    return swapped[::-1, ::-1]


def kernel_partial(padded_first, group_delta, group_size, groups_here):
    rows_here = group_delta.shape[0]
    cols_here = group_delta.shape[1]
    pixels = rows_here * cols_here
    delta_groups = group_delta.reshape(pixels, groups_here, group_size)
    kernel_terms = []
    for row_shift in range(3):
        for col_shift in range(3):
            window = padded_first[
                row_shift : row_shift + rows_here, col_shift : col_shift + cols_here
            ]
            window = window.reshape(pixels, groups_here, group_size)
            kernel_terms.append(
                jnp.einsum("pgi,pgo->gio", window, delta_groups, preferred_element_type=jnp.float32)
            )
    kernel_part = jnp.stack(kernel_terms).reshape(3, 3, groups_here, group_size, group_size)
    kernel_part = jnp.transpose(kernel_part, (0, 1, 3, 2, 4))
    return kernel_part.reshape(3, 3, group_size, groups_here * group_size)


def body(images, first_weight, group_weight, third_weight, out_grad):
    rows_here = images.shape[0]
    cols_here = images.shape[1]
    group_size = group_weight.shape[2]
    first_panel, third_panel = (
        lax.all_gather(first_weight, "chan", axis=0, tiled=True),
        lax.all_gather(third_weight, "chan", axis=0, tiled=True),
    )
    pixels = rows_here * cols_here
    groups_here = group_weight.shape[3] // group_size
    gathered = lax.all_gather(images, "filt", axis=2, tiled=True)
    flat_images = gathered.reshape(pixels, gathered.shape[2])
    pre_first = jnp.dot(flat_images, first_panel, preferred_element_type=jnp.float32)
    act_first = (
        jax.nn.silu(pre_first)
        .astype(jnp.bfloat16)
        .reshape(rows_here, cols_here, first_panel.shape[1])
    )
    padded_first = extended(act_first, (("rows", 0), ("chan", 1)), 1)
    pre_group = group_conv(padded_first, group_weight, groups_here)
    act_group = jax.nn.silu(pre_group).astype(jnp.bfloat16)
    mid_whole = lax.all_gather(act_group, "filt", axis=2, tiled=True)
    flat_mid = mid_whole.reshape(pixels, mid_whole.shape[2])
    third_out = jnp.dot(flat_mid, third_panel, preferred_element_type=jnp.float32)
    own_images = images.reshape(pixels, images.shape[2]).astype(jnp.float32)
    block_out = (own_images + third_out).astype(jnp.bfloat16).reshape(images.shape)
    grad_flat = out_grad.reshape(pixels, out_grad.shape[2])
    mid_terms = lax.dot_general(
        grad_flat, third_panel, (((1,), (1,)), ((), ())), preferred_element_type=jnp.float32
    )
    mid_grad = lax.psum_scatter(
        mid_terms.reshape(rows_here, cols_here, mid_terms.shape[1]),
        "filt",
        scatter_dimension=2,
        tiled=True,
    )
    third_part = lax.dot_general(
        flat_mid, grad_flat, (((0,), (0,)), ((), ())), preferred_element_type=jnp.float32
    )
    group_delta = (mid_grad * silu_slope(pre_group)).astype(jnp.bfloat16)
    padded_delta = extended(group_delta, (("rows", 0), ("chan", 1)), 1)
    first_back = group_conv(
        padded_delta, transposed_kernel(group_weight, group_size, groups_here), groups_here
    )
    kernel_part = kernel_partial(padded_first, group_delta, group_size, groups_here)
    first_delta = (first_back.reshape(pixels, first_back.shape[2]) * silu_slope(pre_first)).astype(
        jnp.bfloat16
    )
    first_part = lax.dot_general(
        flat_images, first_delta, (((0,), (0,)), ((), ())), preferred_element_type=jnp.float32
    )
    input_terms = lax.dot_general(
        first_delta, first_panel, (((1,), (1,)), ((), ())), preferred_element_type=jnp.float32
    )
    back_images = lax.psum_scatter(
        input_terms.reshape(rows_here, cols_here, input_terms.shape[1]).astype(jnp.bfloat16),
        "filt",
        scatter_dimension=2,
        tiled=True,
    ).astype(jnp.float32)
    images_grad = out_grad.astype(jnp.float32) + back_images
    group_grad = lax.psum(kernel_part, ("rows", "chan"))
    first_total, third_total = lax.psum((first_part, third_part), "rows")
    first_grad, third_grad = (
        lax.psum_scatter(first_total, "chan", scatter_dimension=0, tiled=True),
        lax.psum_scatter(third_total, "chan", scatter_dimension=0, tiled=True),
    )
    return (block_out, images_grad, first_grad, group_grad, third_grad)


def solution(mesh):
    in_specs = (
        P("rows", "chan", "filt"),
        P("chan", "filt"),
        P(None, None, None, "filt"),
        P("chan", "filt"),
        P("rows", "chan", "filt"),
    )
    out_specs = (
        P("rows", "chan", "filt"),
        P("rows", "chan", "filt"),
        P("chan", "filt"),
        P(None, None, None, "filt"),
        P("chan", "filt"),
    )
    return jax.shard_map(body, mesh=mesh, in_specs=in_specs, out_specs=out_specs, check_vma=False)
```

profile of v0, /device:TPU:32, one launch (start us, length us, event | category | flops | bytes accessed | tf_op | source)
XLA Modules:
  0.0 700.0 jit_solution(2654013649618200023)
XLA Ops:
  7.2 0.7 all-gather.3.cloned.1.call-update
  7.9 39.6 %all_gather.15 = bf16[1024,256]{1,0:T(8,128)(2,1)S(1)} all-gather(bf16[128,256]{1,0:T(8,128)(2,1)} %param.8), channel_id=1, replica_groups=mesh['rows'=4,'chan'=8,'filt'=8] {'chan'}, dimensions={0}, use_global_device_ids=true | all-gather | bytes 589824 | tf_op jit(solution)/shard_map/all_gather | solution.py:72
  47.5 3.8 fusion.10
  51.4 0.8 copy-done.13
  52.2 36.9 %all_gather.13 = bf16[2048,128]{1,0:T(8,128)(2,1)S(1)} all-gather(bf16[256,128]{1,0:T(8,128)(2,1)S(1)} %copy-done.13), channel_id=1, replica_groups=mesh['rows'=4,'chan'=8,'filt'=8] {'chan'}, dimensions={0}, use_global_device_ids=true | all-gather | bytes 589824 | tf_op jit(solution)/shard_map/all_gather | solution.py:71
  89.1 4.4 multiply_convert_fusion.3
  93.5 2.9 collective-permute-start
  96.4 1.3 collective-permute-start.1
  97.9 0.4 collective-permute-done
  98.4 4.2 collective-permute-done.1
  103.2 3.4 collective-permute-start.2
  106.6 3.2 collective-permute-start.3
  109.8 0.9 shard_map.94
  110.7 8.0 %collective-permute-done.2 = bf16[6,1,128]{1,2,0:T(8,128)(2,1)S(1)} collective-permute-done((bf16[6,1,128]{1,2,0:T(8,128)(2,1)S(1)}, bf16[6,1,128]{1,2,0:T(8,128)(2,1)S(1)}, u32[]{:S(2)}, u32[]{:S(2)}) %collective-permute-start.2) | collective-permute-done | bytes 1568 | tf_op jit(solution)/shard_map/ppermute | solution.py:12
  118.7 10.6 %collective-permute-done.3 = bf16[6,1,128]{1,2,0:T(8,128)(2,1)S(1)} collective-permute-done((bf16[6,1,128]{1,2,0:T(8,128)(2,1)S(1)}, bf16[6,1,128]{1,2,0:T(8,128)(2,1)S(1)}, u32[]{:S(2)}, u32[]{:S(2)}) %collective-permute-start.3) | collective-permute-done | bytes 1568 | tf_op jit(solution)/shard_map/ppermute | solution.py:15
  129.6 0.4 copy-done.6
  130.0 5.8 copy.36
  135.8 9.4 %fusion.13 = f32[1,4,256,4,32]{4,0,3,2,1:T(1,128)S(1)} fusion(bf16[1,6,258,4,32]{4,0,3,2,1:T(2,128)(2,1)} %copy.36, bf16[3,3,32,4,32]{4,3,2,1,0:T(4,128)(2,1)} %shard_map.94), kind=kOutput, calls=%fused_computation.39 | convolution fusion | flops 75497472 | bytes 994304 | tf_op jit(solution)/shard_map/conv_general_dilated | solution.py:26
  145.3 3.5 copy.38
  148.8 1.3 copy.40
  150.2 2.0 multiply_convert_fusion.1
  152.2 3.3 collective-permute-start.4
  155.6 1.3 collective-permute-start.5
  156.9 0.6 collective-permute-done.4
  157.5 4.3 collective-permute-done.5
  161.8 3.5 collective-permute-start.6
  165.3 2.6 collective-permute-start.7
  168.3 0.9 rev.6
  169.2 2.5 collective-permute-done.7
  172.1 5.9 copy.44
  178.0 13.8 %convolution_reduce_fusion = f32[4,256,4,32]{3,2,1,0:T(4,128)S(1)} fusion(bf16[1,6,258,4,32]{4,0,3,2,1:T(2,128)(2,1)} %copy.44, bf16[3,3,32,4,32]{4,3,2,1,0:T(4,128)(2,1)} %rev.6), kind=kOutput, calls=%fused_computation.2 | convolution fusion | flops 75497472 | bytes 994304 | tf_op jit(solution)/shard_map/conv_general_dilated | solution.py:26
  191.8 1.7 reshape.99
  193.5 1.4 multiply_convert_fusion
  194.9 4.0 convolution_bitcast_fusion
  199.0 3.4 convolution_bitcast_fusion.1
  202.4 40.0 %reduce-scatter.9.cloned.1.call-done = f32[256,128]{0,1:T(8,128)} async-done(((f32[2048,128]{0,1:T(8,128)}), f32[256,128]{0,1:T(8,128)}) %reduce-scatter.9.cloned.1.call-update) | async-done | bytes 131088 | tf_op jit(solution)/shard_map/reduce_scatter | solution.py:130
  242.4 44.5 %reduce-scatter.11.cloned.1.call-done = f32[128,256]{1,0:T(8,128)} async-done(((f32[1024,256]{1,0:T(8,128)}), f32[128,256]{1,0:T(8,128)}) %reduce-scatter.11.cloned.1.call-update) | async-done | bytes 131088 | tf_op jit(solution)/shard_map/reduce_scatter | solution.py:131
  286.9 3.2 convolution_convert_fusion
  290.7 0.3 copy-done.8
  291.8 1.2 pad_maximum_fusion.1
  293.4 0.9 copy.48
  294.3 1.8 reshape.85
  296.1 0.9 copy.51
  297.0 1.1 reshape.88
  298.1 0.9 copy.52
  299.1 1.8 reshape.89
  301.2 0.9 copy.55
  302.2 1.1 reshape.91
  303.3 0.9 copy.57
  304.2 1.1 reshape.93
  305.3 0.9 copy.49
  306.2 1.1 reshape.86
  307.3 1.1 fusion.9
  308.9 1.2 fusion.6
  311.1 0.4 copy.58
  311.5 0.9 reshape.95
  312.5 3.2 fusion
  315.6 21.3 %all-reduce.6.cloned.1.call-done = (f32[256,128]{0,1:T(8,128)}, f32[128,256]{1,0:T(8,128)}) async-done(((f32[256,128]{0,1:T(8,128)}, f32[128,256]{1,0:T(8,128)}), (f32[256,128]{0,1:T(8,128)}, f32[128,256]{1,0:T(8,128)})) %all-reduce.6.cloned.1.call-update) | async-done | bytes 262160 | tf_op jit(solution)/shard_map/psum | solution.py:128
  337.0 1.7 copy.60
  338.7 59.3 %reduce-scatter.7.cloned.1.call-done = bf16[4,256,256]{2,1,0:T(8,128)(2,1)} async-done(((bf16[4,256,2048]{2,1,0:T(8,128)(2,1)}), bf16[4,256,256]{2,1,0:T(8,128)(2,1)}) %reduce-scatter.7.cloned.1.call-update) | async-done | bytes 524304 | tf_op jit(solution)/shard_map/reduce_scatter | solution.py:120
  398.0 2.1 convert_add_fusion
  400.1 290.7 %all-reduce.4.cloned.1.call-done = f32[3,3,32,128]{3,2,1,0:T(8,128)} async-done(((f32[3,3,32,128]{3,2,1,0:T(8,128)}), f32[3,3,32,128]{3,2,1,0:T(8,128)}) %all-reduce.4.cloned.1.call-update) | async-done | bytes 147472 | tf_op jit(solution)/shard_map/psum | solution.py:127
  690.9 1.6 copy.78
  692.5 0.7 copy.79
  (74 shorter events, 6.0 us)
Async XLA Ops:
  7.2 81.9 %all-gather.3.cloned.1.call-start = ((), (), s32[]{:S(2)}) async-start(), calls=%async_computation.4 | async-start | bytes 4718592 | tf_op jit(solution)/shard_map/all_gather | solution.py:76
  7.9 142.2 %reduce-scatter.5.cloned.1.call-start = ((), (), s32[]{:S(2)}) async-start(), calls=%async_computation.6 | async-start | bytes 4718592 | tf_op jit(solution)/shard_map/reduce_scatter | solution.py:96
  51.3 0.8 copy-start.13
  51.4 147.6 %all-gather.5.cloned.1.call-start = ((), (), s32[]{:S(2)}) async-start(), calls=%async_computation.5 | async-start | bytes 2359296 | tf_op jit(solution)/shard_map/all_gather | solution.py:87
  89.1 4.4 copy-start
  93.5 16.3 %copy-start.12 = (bf16[3,3,32,128]{3,2,1,0:T(8,128)(2,1)S(1)}, bf16[3,3,32,128]{3,2,1,0:T(8,128)(2,1)}, u32[]{:S(2)}) copy-start(bf16[3,3,32,128]{3,2,1,0:T(8,128)(2,1)} %param.7) | copy-start | bytes 221188
  93.5 4.8 collective-permute-start
  96.4 6.2 collective-permute-start.1
  98.3 4.6 copy-start.7
  102.6 0.6 copy-start.9
  103.2 15.5 %collective-permute-start.2 = (bf16[6,1,128]{1,2,0:T(8,128)(2,1)S(1)}, bf16[6,1,128]{1,2,0:T(8,128)(2,1)S(1)}, u32[]{:S(2)}, u32[]{:S(2)}) collective-permute-start(bf16[6,1,128]{1,2,0:T(8,128)(2,1)S(1)} %get-tuple-element.29), channel_id=1, source_target_pairs={{0,8},{8,16},{16,24},{24,32},{32,40},{40,48},{48,56},{1,9},{9,17},... | collective-permute-start | bytes 4616 | tf_op jit(solution)/shard_map/ppermute | solution.py:12
  106.6 22.7 %collective-permute-start.3 = (bf16[6,1,128]{1,2,0:T(8,128)(2,1)S(1)}, bf16[6,1,128]{1,2,0:T(8,128)(2,1)S(1)}, u32[]{:S(2)}, u32[]{:S(2)}) collective-permute-start(bf16[6,1,128]{1,2,0:T(8,128)(2,1)S(1)} %get-tuple-element.30), channel_id=1, source_target_pairs={{8,0},{16,8},{24,16},{32,24},{40,32},{48,40},{56,48},{9,1},{17,9},... | collective-permute-start | bytes 4616 | tf_op jit(solution)/shard_map/ppermute | solution.py:15
  118.7 17.1 %copy-start.4 = (bf16[6,1,128]{1,2,0:T(8,128)(2,1)}, bf16[6,1,128]{1,2,0:T(8,128)(2,1)S(1)}, u32[]{:S(2)}) copy-start(bf16[6,1,128]{1,2,0:T(8,128)(2,1)S(1)} %collective-permute-done.2) | copy-start | bytes 4612
  129.3 0.7 copy-start.6
  148.8 19.0 %copy-start.3 = (bf16[3,3,32,4,32]{4,3,2,1,0:T(4,128)(2,1)S(1)}, bf16[3,3,32,4,32]{4,3,2,1,0:T(4,128)(2,1)}, u32[]{:S(2)}) copy-start(bf16[3,3,32,4,32]{4,3,2,1,0:T(4,128)(2,1)} %shard_map.94) | copy-start | bytes 221188
  152.2 90.2 %reduce-scatter.9.cloned.1.call-start = ((), (), s32[]{:S(2)}) async-start(), calls=%async_computation.9 | async-start | bytes 1179648 | tf_op jit(solution)/shard_map/reduce_scatter | solution.py:130
  152.2 5.2 collective-permute-start.4
  155.6 6.2 collective-permute-start.5
  161.8 7.4 %collective-permute-start.6 = (bf16[6,1,128]{2,1,0:T(2,128)(2,1)S(1)}, bf16[6,1,128]{2,1,0:T(2,128)(2,1)S(1)}, u32[]{:S(2)}, u32[]{:S(2)}) collective-permute-start(bf16[6,1,128]{2,1,0:T(2,128)(2,1)S(1)} %get-tuple-element.27), channel_id=1, source_target_pairs={{0,8},{8,16},{16,24},{24,32},{32,40},{40,48},{48,56},{1,9},{9,17},... | collective-permute-start | bytes 4616 | tf_op jit(solution)/shard_map/ppermute | solution.py:12
  165.3 6.4 collective-permute-start.7
  194.9 4.1 copy-start.2
  198.9 88.0 %copy-start.1 = (bf16[2048,128]{1,0:T(8,128)(2,1)S(1)}, bf16[2048,128]{1,0:T(8,128)(2,1)}, u32[]{:S(2)}) copy-start(bf16[2048,128]{1,0:T(8,128)(2,1)} %copy-done) | copy-start | bytes 1572868
  198.9 88.0 %reduce-scatter.11.cloned.1.call-start = ((), (), s32[]{:S(2)}) async-start(), calls=%async_computation.10 | async-start | bytes 1179648 | tf_op jit(solution)/shard_map/reduce_scatter | solution.py:131
  202.4 134.6 %all-reduce.6.cloned.1.call-start = ((), (), s32[]{:S(2)}) async-start(), calls=%async_computation.11 | async-start | bytes 524288 | tf_op jit(solution)/shard_map/psum | solution.py:128
  286.9 111.1 %reduce-scatter.7.cloned.1.call-start = ((), (), s32[]{:S(2)}) async-start(), calls=%async_computation.7 | async-start | bytes 4718592 | tf_op jit(solution)/shard_map/reduce_scatter | solution.py:120
  290.2 0.8 copy-start.8
  290.2 0.9 copy-start.10
  290.2 1.6 copy-start.5
  290.2 400.7 %all-reduce.4.cloned.1.call-start = ((), (), s32[]{:S(2)}) async-start(), calls=%async_computation.8 | async-start | bytes 294912 | tf_op jit(solution)/shard_map/psum | solution.py:127
  337.0 355.5 %copy-start.11 = (f32[128,256]{1,0:T(8,128)S(1)}, f32[128,256]{1,0:T(8,128)}, u32[]{:S(2)}) copy-start(f32[128,256]{1,0:T(8,128)} %get-tuple-element.46) | copy-start | bytes 393220
Sparse Core Ops, SparseCore 0:
  9.8 60.3 all-gather.2
  72.7 76.7 reduce-scatter.4
  152.3 42.8 all-gather.4
  199.0 43.3 reduce-scatter.8
  244.8 42.0 reduce-scatter.10
  289.1 47.8 all-reduce.5
  339.7 58.2 reduce-scatter.6
  401.4 289.4 all-reduce.3
where the time goes:
time: 701 us; the launch traced here: 700 us
  waiting for transfers between devices  487 us (69%)
  blocking collectives  76.5 us (11%)
  matrix products  49 us (7%)
  local copies, waits for them, and re-layouts  43.4 us (6%)
  starting transfers between devices  22 us (3%)
  between operations  14.5 us (2%)
  other arithmetic  7.29 us (1%)
    psum x1, waiting for transfers between devices, body(): group_grad = lax.psum(kernel_part, ('rows', 'chan'))  291 us
    reduce_scatter x1, waiting for transfers between devices, body(): lax.psum_scatter(input_terms.reshape(rows_here, cols_here, input_terms.sh...  59.3 us
    reduce_scatter x1, waiting for transfers between devices, body(): lax.psum_scatter(third_total, 'chan', scatter_dimension=0, tiled=True)  44.5 us
    reduce_scatter x1, waiting for transfers between devices, body(): lax.psum_scatter(first_total, 'chan', scatter_dimension=0, tiled=True)  40 us
    all_gather x1, blocking collectives, body(): lax.all_gather(third_weight, 'chan', axis=0, tiled=True)  39.6 us
    all_gather x1, blocking collectives, body(): lax.all_gather(first_weight, 'chan', axis=0, tiled=True)  36.9 us
    conv_general_dilated x2, matrix products, group_conv(): lax.conv_general_dilated(padded[None], kernel, (1, 1), 'VALID', dimension...  23.3 us
    ppermute x4, waiting for transfers between devices, extended(): lax.ppermute(lax.slice_in_dim(block, 0, width, axis=dim), axis, backward)  21.5 us
  transfers between devices with their start and end apart: 16, of which 12 were waited for; matrix products, arithmetic and copies ran while one was open for 13% of the time, Pallas kernels for 0%

commit v1 on v0

--- a/solution.py
+++ b/solution.py
@@ -124,7 +124,7 @@
         tiled=True,
     ).astype(jnp.float32)
     images_grad = out_grad.astype(jnp.float32) + back_images
-    group_grad = lax.psum(kernel_part, ("rows", "chan"))
+    group_grad = lax.psum(lax.psum(kernel_part, "rows"), "chan")
     first_total, third_total = lax.psum((first_part, third_part), "rows")
     first_grad, third_grad = (
         lax.psum_scatter(first_total, "chan", scatter_dimension=0, tiled=True),

time: 701 us -> 493 us (0.70)
  waiting for transfers between devices: 487 us -> 283 us
    psum x1, waiting for transfers between devices: 291 us -> 78.4 us  [body(): group_grad = lax.psum(lax.psum(kernel_part, 'rows'), 'chan')]
    psum x1, waiting for transfers between devices: 21.3 us -> 44.1 us  [body(): first_total, third_total = lax.psum((first_part, third_part), 'rows')]
    reduce_scatter x1, waiting for transfers between devices: 40 us -> 25.5 us  [body(): lax.psum_scatter(first_total, 'chan', scatter_dimension=0, tiled=True)]
  transfers between devices with their start and end apart: 16 -> 16, of which waited for: 12 -> 12; matrix products, arithmetic and copies ran while one was open for 13% -> 18% of each run, Pallas kernels for 0% -> 0%
where the time goes in v1:
time: 493 us; the launch traced here: 489 us
  waiting for transfers between devices  283 us (57%)
  blocking collectives  76.5 us (16%)
  matrix products  49 us (10%)
  local copies, waits for them, and re-layouts  37.7 us (8%)
  starting transfers between devices  22 us (4%)
  between operations  14.6 us (3%)
  other arithmetic  6.36 us (1%)
    psum x1, waiting for transfers between devices, body(): group_grad = lax.psum(lax.psum(kernel_part, 'rows'), 'chan')  78.4 us
    reduce_scatter x1, waiting for transfers between devices, body(): lax.psum_scatter(input_terms.reshape(rows_here, cols_here, input_terms.sh...  59.7 us
    reduce_scatter x1, waiting for transfers between devices, body(): lax.psum_scatter(third_total, 'chan', scatter_dimension=0, tiled=True)  44.3 us
    psum x1, waiting for transfers between devices, body(): first_total, third_total = lax.psum((first_part, third_part), 'rows')  44.1 us
    all_gather x1, blocking collectives, body(): lax.all_gather(third_weight, 'chan', axis=0, tiled=True)  39.6 us
    all_gather x1, blocking collectives, body(): lax.all_gather(first_weight, 'chan', axis=0, tiled=True)  36.9 us
    reduce_scatter x1, waiting for transfers between devices, body(): lax.psum_scatter(first_total, 'chan', scatter_dimension=0, tiled=True)  25.5 us
    conv_general_dilated x2, matrix products, group_conv(): lax.conv_general_dilated(padded[None], kernel, (1, 1), 'VALID', dimension...  23.3 us
  transfers between devices with their start and end apart: 16, of which 12 were waited for; matrix products, arithmetic and copies ran while one was open for 18% of the time, Pallas kernels for 0%

profile of v1, /device:TPU:32, one launch (start us, length us, event | category | flops | bytes accessed | tf_op | source)
XLA Modules:
  0.0 489.4 jit_solution(568401535661509054)
XLA Ops:
  7.2 0.7 all-gather.3.cloned.1.call-update
  7.9 39.6 %all_gather.15 = bf16[1024,256]{1,0:T(8,128)(2,1)S(1)} all-gather(bf16[128,256]{1,0:T(8,128)(2,1)} %param.8), channel_id=1, replica_groups=mesh['rows'=4,'chan'=8,'filt'=8] {'chan'}, dimensions={0}, use_global_device_ids=true | all-gather | bytes 589824 | tf_op jit(solution)/shard_map/all_gather | solution.py:72
  47.5 3.8 fusion.10
  51.4 0.8 copy-done.17
  52.2 36.9 %all_gather.13 = bf16[2048,128]{1,0:T(8,128)(2,1)S(1)} all-gather(bf16[256,128]{1,0:T(8,128)(2,1)S(1)} %copy-done.17), channel_id=1, replica_groups=mesh['rows'=4,'chan'=8,'filt'=8] {'chan'}, dimensions={0}, use_global_device_ids=true | all-gather | bytes 589824 | tf_op jit(solution)/shard_map/all_gather | solution.py:71
  89.1 4.4 multiply_convert_fusion.3
  93.5 2.9 collective-permute-start
  96.4 1.3 collective-permute-start.1
  97.9 0.4 collective-permute-done
  98.4 4.2 collective-permute-done.1
  102.9 0.3 copy-done.13
  103.2 3.4 collective-permute-start.2
  106.6 3.2 collective-permute-start.3
  109.8 0.9 shard_map.94
  110.7 8.0 %collective-permute-done.2 = bf16[6,1,128]{1,2,0:T(8,128)(2,1)S(1)} collective-permute-done((bf16[6,1,128]{1,2,0:T(8,128)(2,1)S(1)}, bf16[6,1,128]{1,2,0:T(8,128)(2,1)S(1)}, u32[]{:S(2)}, u32[]{:S(2)}) %collective-permute-start.2) | collective-permute-done | bytes 1568 | tf_op jit(solution)/shard_map/ppermute | solution.py:12
  118.7 10.6 %collective-permute-done.3 = bf16[6,1,128]{1,2,0:T(8,128)(2,1)S(1)} collective-permute-done((bf16[6,1,128]{1,2,0:T(8,128)(2,1)S(1)}, bf16[6,1,128]{1,2,0:T(8,128)(2,1)S(1)}, u32[]{:S(2)}, u32[]{:S(2)}) %collective-permute-start.3) | collective-permute-done | bytes 1568 | tf_op jit(solution)/shard_map/ppermute | solution.py:15
  129.3 0.3 pad_maximum_fusion
  129.7 0.3 copy-done.8
  130.0 5.8 %copy.36 = bf16[1,6,258,4,32]{4,0,3,2,1:T(2,128)(2,1)} copy(bf16[1,6,258,4,32]{2,4,3,1,0:T(8,128)(2,1)S(1)} %bitcast.121) | data formatting | bytes 792576 | tf_op jit(solution)/shard_map/broadcast_in_dim | solution.py:27
  135.8 9.4 %fusion.13 = f32[1,4,256,4,32]{4,0,3,2,1:T(1,128)S(1)} fusion(bf16[1,6,258,4,32]{4,0,3,2,1:T(2,128)(2,1)} %copy.36, bf16[3,3,32,4,32]{4,3,2,1,0:T(4,128)(2,1)} %shard_map.94), kind=kOutput, calls=%fused_computation.39 | convolution fusion | flops 75497472 | bytes 994304 | tf_op jit(solution)/shard_map/conv_general_dilated | solution.py:26
  145.3 3.5 copy.38
  148.8 1.3 copy.40
  150.1 2.0 multiply_convert_fusion.1
  152.2 3.4 collective-permute-start.4
  155.6 1.3 collective-permute-start.5
  156.9 0.6 collective-permute-done.4
  157.5 4.3 collective-permute-done.5
  161.8 3.3 collective-permute-start.6
  165.1 2.8 collective-permute-start.7
  167.9 0.2 copy.43
  168.3 0.9 rev.6
  169.2 2.3 collective-permute-done.7
  171.6 0.3 copy.42
  171.9 5.9 %copy.44 = bf16[1,6,258,4,32]{4,0,3,2,1:T(2,128)(2,1)} copy(bf16[1,6,258,4,32]{2,4,3,1,0:T(8,128)(2,1)S(1)} %bitcast.120) | data formatting | bytes 792576 | tf_op jit(solution)/shard_map/broadcast_in_dim | solution.py:27
  177.8 13.8 %convolution_reduce_fusion = f32[4,256,4,32]{3,2,1,0:T(4,128)S(1)} fusion(bf16[1,6,258,4,32]{4,0,3,2,1:T(2,128)(2,1)} %copy.44, bf16[3,3,32,4,32]{4,3,2,1,0:T(4,128)(2,1)} %rev.6), kind=kOutput, calls=%fused_computation.2 | convolution fusion | flops 75497472 | bytes 994304 | tf_op jit(solution)/shard_map/conv_general_dilated | solution.py:26
  191.7 1.7 reshape.99
  193.3 1.4 multiply_convert_fusion
  194.8 3.9 convolution_bitcast_fusion
  198.7 0.3 reduce-scatter.11.cloned.1.call-start
  200.0 0.3 pad_maximum_fusion.1
  200.3 0.3 fusion.15
  200.7 0.9 copy.48
  201.6 1.8 reshape.85
  203.6 0.9 reshape.88
  204.7 0.9 reshape.89
  206.2 0.9 reshape.91
  207.9 3.3 convolution_bitcast_fusion.1
  211.7 0.5 copy-done.4
  212.4 1.2 fusion.6
  214.0 1.2 fusion.3
  215.6 0.4 copy.58
  216.0 0.9 reshape.95
  216.9 25.5 %reduce-scatter.9.cloned.1.call-done = f32[256,128]{0,1:T(8,128)} async-done(((f32[2048,128]{0,1:T(8,128)}), f32[256,128]{0,1:T(8,128)}) %reduce-scatter.9.cloned.1.call-update) | async-done | bytes 131088 | tf_op jit(solution)/shard_map/reduce_scatter | solution.py:130
  242.4 44.3 %reduce-scatter.11.cloned.1.call-done = f32[128,256]{1,0:T(8,128)} async-done(((f32[1024,256]{1,0:T(8,128)}), f32[128,256]{1,0:T(8,128)}) %reduce-scatter.11.cloned.1.call-update) | async-done | bytes 131088 | tf_op jit(solution)/shard_map/reduce_scatter | solution.py:131
  286.8 3.2 convolution_convert_fusion
  290.1 1.0 copy-done.10
  291.1 3.1 fusion
  294.2 44.1 %all-reduce.6.cloned.1.call-done = (f32[256,128]{0,1:T(8,128)}, f32[3,3,32,128]{3,2,1,0:T(8,128)}, f32[128,256]{1,0:T(8,128)}) async-done(((f32[256,128]{0,1:T(8,128)}, f32[3,3,32,128]{3,2,1,0:T(8,128)}, f32[128,256]{1,0:T(8,128)}), (f32[256,128]{0,1:T(8,128)}, f32[3,3,32,128]{3,2,1,0:T(8,128)}, f32[128,256]{1,0:T(8,128)})) %all-reduce.6.cloned.1.call-update) | async-done | bytes 409616 | tf_op jit(solution)/shard_map/psum | solution.py:128
  338.4 1.7 copy.60
  340.1 59.7 %reduce-scatter.7.cloned.1.call-done = bf16[4,256,256]{2,1,0:T(8,128)(2,1)} async-done(((bf16[4,256,2048]{2,1,0:T(8,128)(2,1)}), bf16[4,256,256]{2,1,0:T(8,128)(2,1)}) %reduce-scatter.7.cloned.1.call-update) | async-done | bytes 524304 | tf_op jit(solution)/shard_map/reduce_scatter | solution.py:120
  399.8 2.1 convert_add_fusion
  401.9 78.4 %all-reduce.4.cloned.1.call-done = f32[3,3,32,128]{3,2,1,0:T(8,128)} async-done(((f32[3,3,32,128]{3,2,1,0:T(8,128)}), f32[3,3,32,128]{3,2,1,0:T(8,128)}) %all-reduce.4.cloned.1.call-update) | async-done | bytes 147472 | tf_op jit(solution)/shard_map/psum | solution.py:127
  480.3 1.6 copy.79
  481.9 0.7 copy.80
  (82 shorter events, 5.5 us)
Async XLA Ops:
  7.2 81.9 %all-gather.3.cloned.1.call-start = ((), (), s32[]{:S(2)}) async-start(), calls=%async_computation.4 | async-start | bytes 4718592 | tf_op jit(solution)/shard_map/all_gather | solution.py:76
  7.9 142.2 %reduce-scatter.5.cloned.1.call-start = ((), (), s32[]{:S(2)}) async-start(), calls=%async_computation.6 | async-start | bytes 4718592 | tf_op jit(solution)/shard_map/reduce_scatter | solution.py:96
  51.3 0.8 copy-start.17
  51.4 156.5 %all-gather.5.cloned.1.call-start = ((), (), s32[]{:S(2)}) async-start(), calls=%async_computation.5 | async-start | bytes 2359296 | tf_op jit(solution)/shard_map/all_gather | solution.py:87
  89.1 4.4 copy-start
  93.5 16.2 %copy-start.16 = (bf16[3,3,32,128]{3,2,1,0:T(8,128)(2,1)S(1)}, bf16[3,3,32,128]{3,2,1,0:T(8,128)(2,1)}, u32[]{:S(2)}) copy-start(bf16[3,3,32,128]{3,2,1,0:T(8,128)(2,1)} %param.7) | copy-start | bytes 221188
  93.5 4.8 collective-permute-start
  96.4 6.2 %collective-permute-start.1 = (bf16[1,256,128]{2,1,0:T(8,128)(2,1)S(1)}, bf16[1,256,128]{2,1,0:T(8,128)(2,1)S(1)}, u32[]{:S(2)}, u32[]{:S(2)}) collective-permute-start(bf16[1,256,128]{2,1,0:T(8,128)(2,1)S(1)} %get-tuple-element.37), channel_id=1, source_target_pairs={{64,0},{128,64},{192,128},{65,1},{129,65},{193,129},{66,2},{130,66... | collective-permute-start | bytes 196616 | tf_op jit(solution)/shard_map/ppermute | solution.py:15
  98.3 4.6 copy-start.11
  102.6 0.6 copy-start.13
  103.2 15.5 %collective-permute-start.2 = (bf16[6,1,128]{1,2,0:T(8,128)(2,1)S(1)}, bf16[6,1,128]{1,2,0:T(8,128)(2,1)S(1)}, u32[]{:S(2)}, u32[]{:S(2)}) collective-permute-start(bf16[6,1,128]{1,2,0:T(8,128)(2,1)S(1)} %get-tuple-element.30), channel_id=1, source_target_pairs={{0,8},{8,16},{16,24},{24,32},{32,40},{40,48},{48,56},{1,9},{9,17},... | collective-permute-start | bytes 4616 | tf_op jit(solution)/shard_map/ppermute | solution.py:12
  106.6 22.7 %collective-permute-start.3 = (bf16[6,1,128]{1,2,0:T(8,128)(2,1)S(1)}, bf16[6,1,128]{1,2,0:T(8,128)(2,1)S(1)}, u32[]{:S(2)}, u32[]{:S(2)}) collective-permute-start(bf16[6,1,128]{1,2,0:T(8,128)(2,1)S(1)} %get-tuple-element.31), channel_id=1, source_target_pairs={{8,0},{16,8},{24,16},{32,24},{40,32},{48,40},{56,48},{9,1},{17,9},... | collective-permute-start | bytes 4616 | tf_op jit(solution)/shard_map/ppermute | solution.py:15
  118.7 17.1 %copy-start.6 = (bf16[6,1,128]{1,2,0:T(8,128)(2,1)}, bf16[6,1,128]{1,2,0:T(8,128)(2,1)S(1)}, u32[]{:S(2)}) copy-start(bf16[6,1,128]{1,2,0:T(8,128)(2,1)S(1)} %collective-permute-done.2) | copy-start | bytes 4612
  129.3 0.7 copy-start.8
  148.8 19.0 %copy-start.3 = (bf16[3,3,32,4,32]{4,3,2,1,0:T(4,128)(2,1)S(1)}, bf16[3,3,32,4,32]{4,3,2,1,0:T(4,128)(2,1)}, u32[]{:S(2)}) copy-start(bf16[3,3,32,4,32]{4,3,2,1,0:T(4,128)(2,1)} %shard_map.94) | copy-start | bytes 221188
  152.2 90.3 %reduce-scatter.9.cloned.1.call-start = ((), (), s32[]{:S(2)}) async-start(), calls=%async_computation.9 | async-start | bytes 1179648 | tf_op jit(solution)/shard_map/reduce_scatter | solution.py:130
  152.2 5.3 %collective-permute-start.4 = (bf16[1,256,128]{2,1,0:T(8,128)(2,1)S(1)}, bf16[1,256,128]{2,1,0:T(8,128)(2,1)S(1)}, u32[]{:S(2)}, u32[]{:S(2)}) collective-permute-start(bf16[1,256,128]{2,1,0:T(8,128)(2,1)S(1)} %get-tuple-element.34), channel_id=1, source_target_pairs={{0,64},{64,128},{128,192},{1,65},{65,129},{129,193},{2,66},{66,130... | collective-permute-start | bytes 196616 | tf_op jit(solution)/shard_map/ppermute | solution.py:12
  155.6 6.2 %collective-permute-start.5 = (bf16[1,256,128]{2,1,0:T(8,128)(2,1)S(1)}, bf16[1,256,128]{2,1,0:T(8,128)(2,1)S(1)}, u32[]{:S(2)}, u32[]{:S(2)}) collective-permute-start(bf16[1,256,128]{2,1,0:T(8,128)(2,1)S(1)} %get-tuple-element.35), channel_id=1, source_target_pairs={{64,0},{128,64},{192,128},{65,1},{129,65},{193,129},{66,2},{130,66... | collective-permute-start | bytes 196616 | tf_op jit(solution)/shard_map/ppermute | solution.py:15
  161.8 7.4 %collective-permute-start.6 = (bf16[6,1,128]{2,1,0:T(2,128)(2,1)S(1)}, bf16[6,1,128]{2,1,0:T(2,128)(2,1)S(1)}, u32[]{:S(2)}, u32[]{:S(2)}) collective-permute-start(bf16[6,1,128]{2,1,0:T(2,128)(2,1)S(1)} %get-tuple-element.28), channel_id=1, source_target_pairs={{0,8},{8,16},{16,24},{24,32},{32,40},{40,48},{48,56},{1,9},{9,17},... | collective-permute-start | bytes 4616 | tf_op jit(solution)/shard_map/ppermute | solution.py:12
  165.1 6.4 %collective-permute-start.7 = (bf16[6,1,128]{2,1,0:T(2,128)(2,1)S(1)}, bf16[6,1,128]{2,1,0:T(2,128)(2,1)S(1)}, u32[]{:S(2)}, u32[]{:S(2)}) collective-permute-start(bf16[6,1,128]{2,1,0:T(2,128)(2,1)S(1)} %get-tuple-element.29), channel_id=1, source_target_pairs={{8,0},{16,8},{24,16},{32,24},{40,32},{48,40},{56,48},{9,1},{17,9},... | collective-permute-start | bytes 4616 | tf_op jit(solution)/shard_map/ppermute | solution.py:15
  194.7 4.5 copy-start.12
  194.7 4.5 copy-start.14
  198.7 1.3 copy-start.7
  198.7 1.3 copy-start.9
  198.7 88.0 %reduce-scatter.11.cloned.1.call-start = ((), (), s32[]{:S(2)}) async-start(), calls=%async_computation.10 | async-start | bytes 1179648 | tf_op jit(solution)/shard_map/reduce_scatter | solution.py:131
  205.6 2.3 copy-start.2
  207.8 3.5 copy-start.5
  211.2 0.9 copy-start.4
  211.2 127.1 %all-reduce.6.cloned.1.call-start = ((), (), s32[]{:S(2)}) async-start(), calls=%async_computation.11 | async-start | bytes 819200 | tf_op jit(solution)/shard_map/psum | solution.py:128
  213.9 72.9 %copy-start.1 = (bf16[2048,128]{1,0:T(8,128)(2,1)S(1)}, bf16[2048,128]{1,0:T(8,128)(2,1)}, u32[]{:S(2)}) copy-start(bf16[2048,128]{1,0:T(8,128)(2,1)} %copy-done) | copy-start | bytes 1572868
  286.8 113.0 %reduce-scatter.7.cloned.1.call-start = ((), (), s32[]{:S(2)}) async-start(), calls=%async_computation.7 | async-start | bytes 4718592 | tf_op jit(solution)/shard_map/reduce_scatter | solution.py:120
  290.1 1.0 copy-start.10
  290.1 190.2 %all-reduce.4.cloned.1.call-start = ((), (), s32[]{:S(2)}) async-start(), calls=%async_computation.8 | async-start | bytes 294912 | tf_op jit(solution)/shard_map/psum | solution.py:127
  338.4 143.5 %copy-start.15 = (f32[128,256]{1,0:T(8,128)S(1)}, f32[128,256]{1,0:T(8,128)}, u32[]{:S(2)}) copy-start(f32[128,256]{1,0:T(8,128)} %get-tuple-element.47) | copy-start | bytes 393220
Sparse Core Ops, SparseCore 0:
  9.8 60.3 all-gather.2
  72.7 76.6 reduce-scatter.4
  152.3 42.8 all-gather.4
  198.9 43.5 reduce-scatter.8
  244.8 41.9 reduce-scatter.10
  289.7 48.5 all-reduce.5
  341.1 58.7 reduce-scatter.6
  402.6 77.6 all-reduce.3
